TPU v7x, 512 devices: a whole 4x4x16 slice. The times are simulated.
512 devices in a mesh: vocab: 32 (over x, y, core), dp: 16 (over z).
Axes of the slice: x: 4, y: 4, z: 16, core: 2. Of those that a mesh axis runs over, the one named last changes fastest.
Arguments:
- hidden: bfloat16 [2048, 2048], P('dp', 'vocab')
- head_weight: bfloat16 [2048, 65536], P('dp', 'vocab')
- teacher_logits: bfloat16 [2048, 65536], P('dp', 'vocab')
- target_ids: int32 [2048], P('dp'), may hold values from 0 to 65535
- segment_ids: int32 [16, 128], P('dp'), may hold values from 0 to 15, never falling along the last dimension, each value on 1 to 16 neighbouring positions
- pair_order: int32 [16, 16], P('dp'), may hold values from 0 to 15, each once within a row
Outputs:
- hidden_grad: bfloat16 [2048, 2048], P('dp', 'vocab')
- head_grad: float32 [2048, 65536], P('dp', 'vocab')
- loss: float32 [], replicated
Inputs may be any that keep to these rules, and one draw needn't show every extreme that they name: `segment_ids`: in each group the row's sequence number never falls along the rows, and every sequence has 1 to 16 rows. `pair_order`: each group's row is a permutation of its 16 sequences; pair p is entry 2p (chosen) and entry 2p + 1 (rejected).
All inputs are finite; a program needn't handle non-finite values.
Results may differ from a plain program's by a relative error of at most 0.018.
Values may be sent and summed in bfloat16 or wider, within the bound.
No kernel may reach another device: no remote copies, remote signals or barrier semaphores. Data moves between devices by JAX's collectives and lax.ppermute only.
A program may use at most 64 MiB of HBM per device.

v0:
```python
import jax
import jax.numpy as jnp
from jax import lax
from jax.sharding import PartitionSpec as P

dpo_beta = 0.1
dpo_gamma = 4.0


def pair_weights(log_ratio, segments, ordering):
    seq_count = ordering.shape[0]
    labels = lax.broadcasted_iota(jnp.int32, (1, seq_count), 1)
    seq_hot = (segments[:, None] == labels).astype(jnp.float32)
    seq_ratio = jnp.sum(seq_hot * log_ratio[:, None], axis=0)
    chosen = ordering[0::2]
    rejected = ordering[1::2]
    chosen_hot = (chosen[:, None] == labels).astype(jnp.float32)
    rejected_hot = (rejected[:, None] == labels).astype(jnp.float32)
    margin = dpo_beta * (
        jnp.sum(chosen_hot * seq_ratio[None, :], axis=1)
        - jnp.sum(rejected_hot * seq_ratio[None, :], axis=1)
    )
    strength = dpo_gamma * dpo_beta * jax.nn.sigmoid(-margin)
    coeffs = jnp.sum((rejected_hot - chosen_hot) * strength[:, None], axis=0)
    row_weight = jnp.sum(seq_hot * coeffs[None, :], axis=1)
    return (row_weight, jnp.sum(jax.nn.softplus(-margin)))


def on_device(hidden, head_weight, teacher_logits, target_ids, segment_ids, pair_order):
    rows_full = lax.all_gather(hidden, "vocab", axis=1, tiled=True)
    weight_full = lax.all_gather(head_weight, "dp", axis=0, tiled=True)
    student = jnp.dot(rows_full, weight_full, preferred_element_type=jnp.float32)
    teacher = teacher_logits.astype(jnp.float32)
    shard_width = student.shape[1]
    offset = lax.axis_index("vocab") * shard_width
    column = lax.broadcasted_iota(jnp.int32, student.shape, 1) + offset
    is_target = column == target_ids[:, None]
    local_target = jnp.sum(jnp.where(is_target, student, 0.0), axis=1)
    local_tgt_teach = jnp.sum(jnp.where(is_target, teacher, 0.0), axis=1)
    local_max = jnp.max(student, axis=1)
    local_tmax = jnp.max(teacher, axis=1)
    max_student, max_teacher = lax.pmax((local_max, local_tmax), "vocab")
    exp_student = jnp.exp(student - max_student[:, None])
    exp_teacher = jnp.exp(teacher - max_teacher[:, None])
    sum_student, sum_teacher, cross, target_student, target_teacher = lax.psum(
        (
            jnp.sum(exp_student, axis=1),
            jnp.sum(exp_teacher, axis=1),
            jnp.sum(exp_teacher * (teacher - student), axis=1),
            local_target,
            local_tgt_teach,
        ),
        "vocab",
    )
    lse_student = max_student + jnp.log(sum_student)
    lse_teacher = max_teacher + jnp.log(sum_teacher)
    kl_rows = cross / sum_teacher - lse_teacher + lse_student
    log_ratio = target_student - lse_student - (target_teacher - lse_teacher)
    row_weight, dpo_sum = pair_weights(log_ratio, segment_ids[0], pair_order[0])
    group_objective = jnp.sum(kl_rows) + dpo_gamma * dpo_sum
    summed_objective = lax.psum(group_objective, "dp")
    loss_value = summed_objective / (rows_full.shape[0] * lax.axis_size("dp"))
    prob_student = exp_student / sum_student[:, None]
    prob_teacher = exp_teacher / sum_teacher[:, None]
    logit_grad = (
        prob_student
        - prob_teacher
        + row_weight[:, None] * (is_target.astype(jnp.float32) - prob_student)
    ).astype(jnp.bfloat16)
    hidden_term = lax.dot_general(
        logit_grad, weight_full, (((1,), (1,)), ((), ())), preferred_element_type=jnp.float32
    )
    hidden_grad = lax.psum_scatter(
        hidden_term.astype(jnp.bfloat16), "vocab", scatter_dimension=1, tiled=True
    )
    grad_cols = lax.all_to_all(rows_full, "dp", split_axis=1, concat_axis=0, tiled=True)
    head_grad = lax.dot_general(
        grad_cols,
        lax.all_gather(logit_grad, "dp", axis=0, tiled=True),
        (((0,), (0,)), ((), ())),
        preferred_element_type=jnp.float32,
    )
    return (hidden_grad, head_grad, loss_value)


def solution(mesh):
    return jax.shard_map(
        on_device,
        mesh=mesh,
        in_specs=(
            P("dp", "vocab"),
            P("dp", "vocab"),
            P("dp", "vocab"),
            P("dp"),
            P("dp", None),
            P("dp", None),
        ),
        out_specs=(P("dp", "vocab"), P("dp", "vocab"), P()),
        check_vma=False,
    )
```

profile of v0, /device:TPU:2, one launch (start us, length us, event | category | flops | bytes accessed | tf_op | source)
XLA Modules:
  0.0 486.9 jit_solution(1537256044486397161)
XLA Ops:
  7.2 0.7 all-gather.3.cloned.1.call-update
  8.0 0.8 slice.7
  8.8 0.7 slice.6
  9.5 1.2 reduce_max.24
  10.7 29.9 %all_gather.9 = bf16[128,2048]{0,1:T(8,128)(2,1)} all-gather(bf16[128,64]{0,1:T(8,128)(2,1)} %param.6), channel_id=1, replica_groups=mesh['vocab'=32,'dp'=16] {'vocab'}, dimensions={1}, use_global_device_ids=true | all-gather | bytes 540672 | tf_op jit(solution)/shard_map/all_gather | solution.py:30
  40.6 79.9 %all-gather.3.cloned.1.call-done = bf16[2048,2048]{1,0:T(8,128)(2,1)} async-done(((bf16[128,2048]{1,0:T(8,128)(2,1)}), bf16[2048,2048]{1,0:T(8,128)(2,1)}) %all-gather.3.cloned.1.call-update) | async-done | bytes 8388624 | tf_op jit(solution)/shard_map/all_gather | solution.py:31
  120.5 4.9 %fusion.14 = (f32[128]{0:T(128)S(1)}, f32[128,2048]{1,0:T(8,128)S(1)}) fusion(bf16[128,2048]{0,1:T(8,128)(2,1)} %all_gather.9, bf16[2048,2048]{1,0:T(8,128)(2,1)} %all-gather.3.cloned.1.call-done), kind=kOutput, calls=%fused_computation.38 | convolution fusion | flops 1074003840 | bytes 9961984 | tf_op jit(solution)/shard_map/dot_general | solution.py:32
  125.4 56.2 %all-reduce.1 = (f32[128]{0:T(128)S(1)}, f32[128]{0:T(128)S(1)}) all-reduce(bf16[128]{0:T(256)(128)(2,1)S(1)} %reduce_max.24, f32[128]{0:T(128)S(1)} %get-tuple-element.33), channel_id=1, replica_groups=mesh['vocab'=32,'dp'=16] {'vocab'}, use_global_device_ids=true, to_apply=%region_5.6 | all-reduce | flops 256 | bytes 1792 | tf_op jit(solution)/shard_map/pmax | solution.py:42
  181.6 0.8 fusion.6
  182.4 56.8 %all-reduce = (f32[128]{0:T(128)S(1)}, f32[128]{0:T(128)S(1)}, f32[128]{0:T(128)S(1)}, f32[128]{0:T(128)S(1)}, f32[128]{0:T(128)S(1)}) all-reduce(f32[128]{0:T(128)S(1)} %get-tuple-element.18, f32[128]{0:T(128)S(1)} %get-tuple-element.16, f32[128]{0:T(128)S(1)} %get-tuple-element.19, ...), channel_id=1, replica_groups=mesh['vocab'=32,'dp'=16] {'vocab'}, use_global_device_ids=true, to_apply=%region_11.12 | all-reduce | flops 640 | bytes 5120 | tf_op jit(solution)/shard_map/psum | solution.py:45
  239.2 0.6 add_reduce_fusion
  239.9 0.1 select_reduce_fusion.1
  240.0 0.2 select_reduce_fusion.2
  240.2 0.6 fusion.13
  241.0 1.4 fusion.11
  242.4 8.9 %all-to-all-start = ((bf16[128,16,128]{0,2,1:T(8,128)(2,1)}), bf16[128,16,128]{0,2,1:T(8,128)(2,1)S(1)}, u32[]{:S(2)}, u32[]{:S(2)}) async-start(bf16[128,16,128]{0,2,1:T(8,128)(2,1)} %bitcast.2), calls=%async_computation.1 | async-start | bytes 1048576 | tf_op jit(solution)/shard_map/all_to_all | solution.py:76
  251.4 6.7 %convolution_convert_fusion = bf16[128,2048]{0,1:T(8,128)(2,1)} fusion(bf16[128,2048]{1,0:T(8,128)(2,1)} %fusion.11, bf16[2048,2048]{1,0:T(8,128)(2,1)} %all-gather.3.cloned.1.call-done), kind=kOutput, calls=%fused_computation.1 | convolution fusion | flops 1074003968 | bytes 9437184 | tf_op jit(solution)/shard_map/dot_general | solution.py:70
  259.3 21.5 %all-to-all-done = bf16[128,16,128]{0,2,1:T(8,128)(2,1)S(1)} async-done(((bf16[128,16,128]{0,2,1:T(8,128)(2,1)}), bf16[128,16,128]{0,2,1:T(8,128)(2,1)S(1)}, u32[]{:S(2)}, u32[]{:S(2)}) %all-to-all-start) | async-done | bytes 524320 | tf_op jit(solution)/shard_map/all_to_all | solution.py:76
  280.9 0.3 copy.13
  281.1 32.6 %psum.47 = f32[]{:T(128)} all-reduce(f32[]{:T(128)S(6)} %add.55), channel_id=1, replica_groups=mesh['vocab'=32,'dp'=16] {'dp'}, use_global_device_ids=true, to_apply=%region_22.23 | all-reduce | flops 1 | bytes 8 | tf_op jit(solution)/shard_map/psum | solution.py:61
  314.4 48.8 %all-gather.5.cloned.1.call-done = bf16[2048,2048]{1,0:T(8,128)(2,1)} async-done(((bf16[128,2048]{1,0:T(8,128)(2,1)}), bf16[2048,2048]{1,0:T(8,128)(2,1)}) %all-gather.5.cloned.1.call-update) | async-done | bytes 8388624 | tf_op jit(solution)/shard_map/all_gather | solution.py:79
  363.2 5.8 %convolution_bitcast_fusion = f32[128,2048]{0,1:T(8,128)S(1)} fusion(bf16[2048,2048]{1,0:T(8,128)(2,1)} %all-gather.5.cloned.1.call-done, bf16[2048,128]{1,0:T(8,128)(2,1)S(1)} %bitcast.14), kind=kOutput, calls=%fused_computation | convolution fusion | flops 1073741824 | bytes 9961472 | tf_op jit(solution)/shard_map/dot_general | solution.py:77
  369.0 1.3 copy.14
  370.3 109.0 %reduce-scatter.2.cloned.1.call-done = bf16[128,64]{0,1:T(8,128)(2,1)} async-done(((bf16[128,2048]{0,1:T(8,128)(2,1)}), bf16[128,64]{0,1:T(8,128)(2,1)}) %reduce-scatter.2.cloned.1.call-update) | async-done | bytes 16400 | tf_op jit(solution)/shard_map/reduce_scatter | solution.py:73
  (14 shorter events, 0.3 us)
Async XLA Ops:
  7.2 113.3 %all-gather.3.cloned.1.call-start = ((), (), s32[]{:S(2)}) async-start(), calls=%async_computation.2 | async-start | bytes 8912896 | tf_op jit(solution)/shard_map/all_gather | solution.py:31
  7.9 173.7 %copy-start = (bf16[128,2048]{1,0:T(8,128)(2,1)S(1)}, bf16[128,2048]{1,0:T(8,128)(2,1)}, u32[]{:S(2)}) copy-start(bf16[128,2048]{1,0:T(8,128)(2,1)} %param.8) | copy-start | bytes 1572868
  7.9 173.7 %copy-start.1 = (s32[128]{0:T(128)S(1)}, s32[128]{0:T(128)}, u32[]{:S(2)}) copy-start(s32[128]{0:T(128)} %param.9) | copy-start | bytes 1540
  7.9 355.3 %all-gather.5.cloned.1.call-start = ((), (), s32[]{:S(2)}) async-start(), calls=%async_computation.4 | async-start | bytes 8912896 | tf_op jit(solution)/shard_map/all_gather | solution.py:79
  40.6 199.2 %copy-start.2 = (s32[1,128]{1,0:T(1,128)S(1)}, s32[1,128]{1,0:T(1,128)}, u32[]{:S(2)}) copy-start(s32[1,128]{1,0:T(1,128)} %param.10) | copy-start | bytes 1540
  242.4 38.4 %all-to-all-start = ((bf16[128,16,128]{0,2,1:T(8,128)(2,1)}), bf16[128,16,128]{0,2,1:T(8,128)(2,1)S(1)}, u32[]{:S(2)}, u32[]{:S(2)}) async-start(bf16[128,16,128]{0,2,1:T(8,128)(2,1)} %bitcast.2), calls=%async_computation.1 | async-start | bytes 1048576 | tf_op jit(solution)/shard_map/all_to_all | solution.py:76
  251.3 227.9 %reduce-scatter.2.cloned.1.call-start = ((), (), s32[]{:S(2)}) async-start(), calls=%async_computation.3 | async-start | bytes 540672 | tf_op jit(solution)/shard_map/reduce_scatter | solution.py:73
Sparse Core Ops, SparseCore 0:
  10.1 110.3 all-gather.2
  242.6 120.6 all-gather.4
  368.1 111.0 reduce-scatter.1
where the time goes:
time: 487 us
  waiting for transfers between devices  260 us (53%)
  blocking collectives  175 us (36%)
  matrix products  17.4 us (4%)
  between operations  16.8 us (3%)
  starting transfers between devices  9 us (2%)
  other arithmetic  5.2 us (1%)
    reduce_scatter x1, waiting for transfers between devices, on_device(): lax.psum_scatter(hidden_term.astype(jnp.bfloat16), 'vocab', scatter_dimen...  109 us
    all_gather x1, waiting for transfers between devices, on_device(): weight_full = lax.all_gather(head_weight, 'dp', axis=0, tiled=True)  79.9 us
    psum x1, blocking collectives, on_device(): lax.psum((jnp.sum(exp_student, axis=1), jnp.sum(exp_teacher, axis=1), jnp...  56.8 us
    pmax x1, blocking collectives, on_device(): max_student, max_teacher = lax.pmax((local_max, local_tmax), 'vocab')  56.2 us
    all_gather x1, waiting for transfers between devices, on_device(): lax.all_gather(logit_grad, 'dp', axis=0, tiled=True)  48.8 us
    psum x1, blocking collectives, on_device(): summed_objective = lax.psum(group_objective, 'dp')  32.6 us
    all_gather x1, blocking collectives, on_device(): rows_full = lax.all_gather(hidden, 'vocab', axis=1, tiled=True)  29.9 us
    all_to_all x1, waiting for transfers between devices, on_device(): lax.all_to_all(rows_full, 'dp', split_axis=1, concat_axis=0, tiled=True)  21.5 us
  transfers between devices with their start and end apart: 4, of which 4 were waited for; matrix products, arithmetic and copies ran while one was open for 3% of the time, Pallas kernels for 0%

commit v1 on v0

--- a/solution.py
+++ b/solution.py
@@ -28,7 +28,9 @@
 
 def on_device(hidden, head_weight, teacher_logits, target_ids, segment_ids, pair_order):
     rows_full = lax.all_gather(hidden, "vocab", axis=1, tiled=True)
-    weight_full = lax.all_gather(head_weight, "dp", axis=0, tiled=True)
+    weight_full = jnp.concatenate(
+        lax.all_to_all(jnp.stack([head_weight] * lax.axis_size("dp")), "dp", 0, 0), axis=0
+    )
     student = jnp.dot(rows_full, weight_full, preferred_element_type=jnp.float32)
     teacher = teacher_logits.astype(jnp.float32)
     shard_width = student.shape[1]

time: 487 us -> 671 us (1.38)
  the two profiles are of different devices: /device:TPU:2 before, /device:TPU:1 now
where the time goes in v1:
time: 671 us; the launch traced here: 670 us
  waiting for transfers between devices  405 us (60%)
  blocking collectives  190 us (28%)
  starting transfers between devices  27.3 us (4%)
  between operations  18.5 us (3%)
  matrix products  17.6 us (3%)
  local copies, waits for them, and re-layouts  7.12 us (1%)
    all_to_all x1, waiting for transfers between devices, on_device(): lax.all_to_all(jnp.stack([head_weight] * lax.axis_size('dp')), 'dp', 0, 0)  333 us
    psum x1, blocking collectives, on_device(): lax.psum((jnp.sum(exp_student, axis=1), jnp.sum(exp_teacher, axis=1), jnp...  66.3 us
    pmax x1, blocking collectives, on_device(): max_student, max_teacher = lax.pmax((local_max, local_tmax), 'vocab')  64.7 us
    all_gather x1, waiting for transfers between devices, on_device(): lax.all_gather(logit_grad, 'dp', axis=0, tiled=True)  50.9 us
    psum x1, blocking collectives, on_device(): summed_objective = lax.psum(group_objective, 'dp')  31.1 us
    all_gather x1, blocking collectives, on_device(): rows_full = lax.all_gather(hidden, 'vocab', axis=1, tiled=True)  28.1 us
    all_to_all x1, waiting for transfers between devices, on_device(): lax.all_to_all(rows_full, 'dp', split_axis=1, concat_axis=0, tiled=True)  21.3 us
    all_to_all x1, starting transfers between devices, on_device(): lax.all_to_all(jnp.stack([head_weight] * lax.axis_size('dp')), 'dp', 0, 0)  15.9 us
  transfers between devices with their start and end apart: 4, of which 3 were waited for; matrix products, arithmetic and copies ran while one was open for 2% of the time, Pallas kernels for 0%

profile of v1, /device:TPU:1, one launch (start us, length us, event | category | flops | bytes accessed | tf_op | source)
XLA Modules:
  0.0 670.2 jit_solution(5568163110719790844)
XLA Ops:
  8.0 5.3 stack.2
  13.3 15.9 %all-to-all-start = ((bf16[16,128,2048]{2,1,0:T(8,128)(2,1)}), bf16[16,128,2048]{2,1,0:T(8,128)(2,1)}, u32[]{:S(2)}, u32[]{:S(2)}) async-start(bf16[16,128,2048]{2,1,0:T(8,128)(2,1)} %stack.2), calls=%async_computation | async-start | bytes 16777216 | tf_op jit(solution)/shard_map/all_to_all | solution.py:32
  29.3 0.1 slice.6
  29.4 0.1 slice.7
  29.5 0.2 reduce_max.24
  29.7 28.1 %all_gather.6 = bf16[128,2048]{0,1:T(8,128)(2,1)} all-gather(bf16[128,64]{0,1:T(8,128)(2,1)S(1)} %copy-done.1), channel_id=1, replica_groups=mesh['vocab'=32,'dp'=16] {'vocab'}, dimensions={1}, use_global_device_ids=true | all-gather | bytes 540672 | tf_op jit(solution)/shard_map/all_gather | solution.py:30
  57.8 333.0 %all-to-all-done = bf16[16,128,2048]{2,1,0:T(8,128)(2,1)} async-done(((bf16[16,128,2048]{2,1,0:T(8,128)(2,1)}), bf16[16,128,2048]{2,1,0:T(8,128)(2,1)}, u32[]{:S(2)}, u32[]{:S(2)}) %all-to-all-start) | async-done | bytes 8388640 | tf_op jit(solution)/shard_map/all_to_all | solution.py:32
  390.8 4.9 fusion.14
  395.7 64.7 %all-reduce.1 = (f32[128]{0:T(128)S(1)}, f32[128]{0:T(128)S(1)}) all-reduce(bf16[128]{0:T(256)(128)(2,1)S(1)} %reduce_max.24, f32[128]{0:T(128)S(1)} %get-tuple-element.33), channel_id=1, replica_groups=mesh['vocab'=32,'dp'=16] {'vocab'}, use_global_device_ids=true, to_apply=%region_5.6 | all-reduce | flops 256 | bytes 1792 | tf_op jit(solution)/shard_map/pmax | solution.py:44
  460.5 0.8 fusion.6
  461.3 66.3 %all-reduce = (f32[128]{0:T(128)S(1)}, f32[128]{0:T(128)S(1)}, f32[128]{0:T(128)S(1)}, f32[128]{0:T(128)S(1)}, f32[128]{0:T(128)S(1)}) all-reduce(f32[128]{0:T(128)S(1)} %get-tuple-element.18, f32[128]{0:T(128)S(1)} %get-tuple-element.16, f32[128]{0:T(128)S(1)} %get-tuple-element.19, ...), channel_id=1, replica_groups=mesh['vocab'=32,'dp'=16] {'vocab'}, use_global_device_ids=true, to_apply=%region_11.12 | all-reduce | flops 640 | bytes 5120 | tf_op jit(solution)/shard_map/psum | solution.py:47
  527.6 0.6 add_reduce_fusion
  528.2 0.1 select_reduce_fusion.1
  528.3 0.2 select_reduce_fusion.2
  528.5 0.6 fusion.13
  529.4 1.4 fusion.11
  530.8 11.3 %all-to-all-start.1 = ((bf16[128,16,128]{0,2,1:T(8,128)(2,1)}), bf16[128,16,128]{0,2,1:T(8,128)(2,1)S(1)}, u32[]{:S(2)}, u32[]{:S(2)}) async-start(bf16[128,16,128]{0,2,1:T(8,128)(2,1)} %bitcast.3), calls=%async_computation.2 | async-start | bytes 1048576 | tf_op jit(solution)/shard_map/all_to_all | solution.py:78
  542.2 6.9 %convolution_convert_fusion = bf16[128,2048]{0,1:T(8,128)(2,1)} fusion(bf16[128,2048]{1,0:T(8,128)(2,1)} %fusion.11, bf16[2048,2048]{1,0:T(8,128)(2,1)} %bitcast), kind=kOutput, calls=%fused_computation.1 | convolution fusion | flops 1074003968 | bytes 9437184 | tf_op jit(solution)/shard_map/dot_general | solution.py:72
  550.3 21.3 %all-to-all-done.1 = bf16[128,16,128]{0,2,1:T(8,128)(2,1)S(1)} async-done(((bf16[128,16,128]{0,2,1:T(8,128)(2,1)}), bf16[128,16,128]{0,2,1:T(8,128)(2,1)S(1)}, u32[]{:S(2)}, u32[]{:S(2)}) %all-to-all-start.1) | async-done | bytes 524320 | tf_op jit(solution)/shard_map/all_to_all | solution.py:78
  571.6 0.3 copy.13
  571.9 31.1 %psum.47 = f32[]{:T(128)} all-reduce(f32[]{:T(128)S(6)} %add.55), channel_id=1, replica_groups=mesh['vocab'=32,'dp'=16] {'dp'}, use_global_device_ids=true, to_apply=%region_22.23 | all-reduce | flops 1 | bytes 8 | tf_op jit(solution)/shard_map/psum | solution.py:63
  603.7 50.9 %all-gather.2.cloned.1.call-done = bf16[2048,2048]{1,0:T(8,128)(2,1)} async-done(((bf16[128,2048]{1,0:T(8,128)(2,1)}), bf16[2048,2048]{1,0:T(8,128)(2,1)}) %all-gather.2.cloned.1.call-update) | async-done | bytes 8388624 | tf_op jit(solution)/shard_map/all_gather | solution.py:81
  654.5 5.8 convolution_bitcast_fusion
  660.3 1.3 copy.14
  (18 shorter events, 0.3 us)
Async XLA Ops:
  13.3 16.0 %copy-start.3 = (s32[1,16]{1,0:T(1,128)S(1)}, s32[1,16]{1,0:T(1,128)}, u32[]{:S(2)}) copy-start(s32[1,16]{1,0:T(1,128)} %param.11) | copy-start | bytes 196
  13.3 16.2 %copy-start = (bf16[128,2048]{1,0:T(8,128)(2,1)S(1)}, bf16[128,2048]{1,0:T(8,128)(2,1)}, u32[]{:S(2)}) copy-start(bf16[128,2048]{1,0:T(8,128)(2,1)} %param.8) | copy-start | bytes 1572868
  13.3 16.4 %copy-start.1 = (bf16[128,64]{0,1:T(8,128)(2,1)S(1)}, bf16[128,64]{0,1:T(8,128)(2,1)}, u32[]{:S(2)}) copy-start(bf16[128,64]{0,1:T(8,128)(2,1)} %param.6) | copy-start | bytes 49156
  13.3 377.5 %all-to-all-start = ((bf16[16,128,2048]{2,1,0:T(8,128)(2,1)}), bf16[16,128,2048]{2,1,0:T(8,128)(2,1)}, u32[]{:S(2)}, u32[]{:S(2)}) async-start(bf16[16,128,2048]{2,1,0:T(8,128)(2,1)} %stack.2), calls=%async_computation | async-start | bytes 16777216 | tf_op jit(solution)/shard_map/all_to_all | solution.py:32
  29.3 431.2 %copy-start.2 = (s32[128]{0:T(128)S(1)}, s32[128]{0:T(128)}, u32[]{:S(2)}) copy-start(s32[128]{0:T(128)} %param.9) | copy-start | bytes 1540
  29.3 625.2 %all-gather.2.cloned.1.call-start = ((), (), s32[]{:S(2)}) async-start(), calls=%async_computation.4 | async-start | bytes 8912896 | tf_op jit(solution)/shard_map/all_gather | solution.py:81
  390.8 137.4 %copy-start.4 = (s32[1,128]{1,0:T(1,128)S(1)}, s32[1,128]{1,0:T(1,128)}, u32[]{:S(2)}) copy-start(s32[1,128]{1,0:T(1,128)} %param.10) | copy-start | bytes 1540
  530.8 40.8 %all-to-all-start.1 = ((bf16[128,16,128]{0,2,1:T(8,128)(2,1)}), bf16[128,16,128]{0,2,1:T(8,128)(2,1)S(1)}, u32[]{:S(2)}, u32[]{:S(2)}) async-start(bf16[128,16,128]{0,2,1:T(8,128)(2,1)} %bitcast.3), calls=%async_computation.2 | async-start | bytes 1048576 | tf_op jit(solution)/shard_map/all_to_all | solution.py:78
  542.1 119.4 %reduce-scatter.2.cloned.1.call-start = ((), (), s32[]{:S(2)}) async-start(), calls=%async_computation.3 | async-start | bytes 540672 | tf_op jit(solution)/shard_map/reduce_scatter | solution.py:75
Sparse Core Ops, SparseCore 0:
  530.9 123.5 all-gather.1
Sparse Core Ops, SparseCore 1:
  549.2 95.1 reduce-scatter.1
